TPU v7x, 32 devices: a whole 2x2x4 slice. The times are simulated.
32 devices in a mesh: wide: 8 (over y, x, core), narrow: 4 (over z).
Axes of the slice: x: 2, y: 2, z: 4, core: 2. Of those that a mesh axis runs over, the one named last changes fastest.
Arguments:
- pixels: bfloat16 [32, 32, 256, 768], P('wide', 'narrow')
- coarse_pixels: bfloat16 [128, 128, 768], P('wide', 'narrow')
- unsure: int32 [32, 32], P('wide', 'narrow'), may hold values from 0 to 1, as said below
- patch_weight: bfloat16 [768, 1024], replicated, may hold values from -0.21875 to 0.21875
- position: bfloat16 [256, 1024], replicated, may hold values from -3 to 3
- qkv_weight: bfloat16 [1024, 3072], replicated
- out_weight: bfloat16 [1024, 1024], replicated, may hold values from -0.1875 to 0.1875
- join_weight: bfloat16 [1024, 1024], replicated, may hold values from -0.1875 to 0.1875
- gain_attn: float32 [1024], replicated, may hold values from 0.25 to 1.75
- gain_head: float32 [1024], replicated, may hold values from 0.25 to 1.75
- head_weight: bfloat16 [1024, 16], replicated, may hold values from -0.1875 to 0.1875
Outputs:
- logits: bfloat16 [32, 32, 16, 256], P('wide', 'narrow')
Inputs may be any that keep to these rules, and one draw needn't show every extreme that they name: `unsure`: A device holds at most 25 flagged tiles, and in every column of devices along wide one device holds exactly that many; the devices of one column along wide hold 7 * 8 flagged tiles together.
All inputs are finite; a program needn't handle non-finite values.
Results may differ from a plain program's by a relative error of at most 0.01.
Values may be sent and summed in bfloat16 or wider, within the bound.
A program may use at most 320 MiB of HBM per device.

v0:
```python
import jax
import jax.numpy as jnp
from jax import lax
from jax.sharding import PartitionSpec as P

D = 1024
HEADS = 16
HD = 64
PD = 768
CLASSES = 16
TS = 16
TT = 256
CS = 4
UNSURE_MOST = 25
RECV = 7


EPS = 1e-06


def padded(cells, sides, width):
    for axis, dim in sides:
        count = lax.axis_size(axis)
        ends = count - 1
        head = lax.slice_in_dim(cells, 0, width, axis=dim)
        tail = lax.slice_in_dim(cells, cells.shape[dim] - width, cells.shape[dim], axis=dim)
        cells = jnp.concatenate(
            [
                lax.ppermute(tail, axis, [(i, (i + 1) % count) for i in range(ends)]),
                cells,
                lax.ppermute(head, axis, [((i + 1) % count, i) for i in range(ends)]),
            ],
            axis=dim,
        )
    return cells


def carried_in(x, axis, combine, identity):
    count, position = (lax.axis_size(axis), lax.axis_index(axis))
    everything = lax.all_gather(x, axis)
    start = jnp.broadcast_to(jnp.asarray(identity, x.dtype), x.shape)

    def step(k, before):
        reached = k < position
        new = combine(before, everything[k])
        return jnp.where(reached, new, before)

    return lax.fori_loop(0, count, step, start)


def interp_table():
    fine = jnp.arange(TS, dtype=jnp.int32)
    eighths = 2 * fine - 3
    lower = eighths // 8
    frac = (eighths - 8 * lower).astype(jnp.float32) / 8.0
    column = jnp.arange(CS + 2, dtype=jnp.int32)
    left = (column[None, :] == (lower + 1)[:, None]).astype(jnp.float32)
    right = (column[None, :] == (lower + 2)[:, None]).astype(jnp.float32)
    return left * (1.0 - frac)[:, None] + right * frac[:, None]


def layer_norm(values, gain):
    center = values - jnp.mean(values, axis=-1, keepdims=True)
    spread = jnp.mean(center * center, axis=-1, keepdims=True)
    return center * lax.rsqrt(spread + EPS) * gain


def attend(tokens, gain_attn, qkv_weight, out_weight):
    count = tokens.shape[0]
    normed = layer_norm(tokens, gain_attn).astype(jnp.bfloat16).reshape(-1, D)
    packed = jnp.dot(normed, qkv_weight, preferred_element_type=jnp.float32).astype(jnp.bfloat16)
    packed = packed.reshape(count, TT, 3 * D)

    def one_head(head_index):
        queries = lax.dynamic_slice_in_dim(packed, head_index * HD, HD, 2)
        key_rows = lax.dynamic_slice_in_dim(packed, D + head_index * HD, HD, 2)
        value_rows = lax.dynamic_slice_in_dim(packed, 2 * D + head_index * HD, HD, 2)
        scores = jnp.einsum(
            "nqd,nkd->nqk", queries, key_rows, preferred_element_type=jnp.float32
        ) * HD ** (-0.5)
        weights = jax.nn.softmax(scores, axis=-1).astype(jnp.bfloat16)
        return jnp.einsum(
            "nqk,nkd->nqd", weights, value_rows, preferred_element_type=jnp.float32
        ).astype(jnp.bfloat16)

    heads_out = lax.map(one_head, jnp.arange(HEADS, dtype=jnp.int32))
    mixed = heads_out.transpose(1, 2, 0, 3).reshape(-1, D)
    return tokens + jnp.dot(mixed, out_weight, preferred_element_type=jnp.float32).reshape(
        count, TT, D
    )


def add_counts(earlier, later):
    return earlier + later


def per_device(
    pixels,
    coarse_pixels,
    unsure,
    patch_weight,
    position,
    qkv_weight,
    out_weight,
    join_weight,
    gain_attn,
    gain_head,
    head_weight,
):
    highest = lax.Precision.HIGHEST
    table = interp_table()
    tile_rows, tile_cols = unsure.shape
    tile_count = tile_rows * tile_cols
    coarse_rows, coarse_cols = (coarse_pixels.shape[0], coarse_pixels.shape[1])
    win_rows = coarse_rows // TS
    win_cols = coarse_cols // TS
    patches = (
        coarse_pixels.reshape(win_rows, TS, win_cols, TS, PD)
        .transpose(0, 2, 1, 3, 4)
        .reshape(-1, PD)
    )
    embed = jnp.dot(patches, patch_weight, preferred_element_type=jnp.float32).reshape(-1, TT, D)
    embed = embed + position.astype(jnp.float32)
    glanced = attend(embed, gain_attn, qkv_weight, out_weight).astype(jnp.bfloat16)
    features = (
        glanced.reshape(win_rows, win_cols, TS, TS, D)
        .transpose(0, 2, 1, 3, 4)
        .reshape(coarse_rows, coarse_cols, D)
    )
    bordered = padded(features, (("wide", 0), ("narrow", 1)), 1)
    wide_pos = lax.axis_index("wide")
    wide_len = lax.axis_size("wide")
    narrow_pos = lax.axis_index("narrow")
    narrow_len = lax.axis_size("narrow")
    top_row = jnp.where(wide_pos == 0, bordered[1:2], bordered[0:1])
    bottom_row = jnp.where(wide_pos == wide_len - 1, bordered[-2:-1], bordered[-1:])
    bordered = jnp.concatenate([top_row, bordered[1:-1], bottom_row], axis=0)
    left_col = jnp.where(narrow_pos == 0, bordered[:, 1:2], bordered[:, 0:1])
    right_col = jnp.where(narrow_pos == narrow_len - 1, bordered[:, -2:-1], bordered[:, -1:])
    bordered = jnp.concatenate([left_col, bordered[:, 1:-1], right_col], axis=1)
    head_input = (
        layer_norm(bordered.astype(jnp.float32), gain_head).astype(jnp.bfloat16).reshape(-1, D)
    )
    coarse_logits = jnp.dot(head_input, head_weight, preferred_element_type=jnp.float32)
    coarse_logits = coarse_logits.reshape(coarse_rows + 2, coarse_cols + 2, CLASSES)
    row_index = (
        jnp.arange(tile_rows, dtype=jnp.int32)[:, None] * CS
        + jnp.arange(CS + 2, dtype=jnp.int32)[None, :]
    ).reshape(-1)
    col_index = (
        jnp.arange(tile_cols, dtype=jnp.int32)[:, None] * CS
        + jnp.arange(CS + 2, dtype=jnp.int32)[None, :]
    ).reshape(-1)
    tile_logits = jnp.take(jnp.take(coarse_logits, row_index, axis=0), col_index, axis=1)
    tile_logits = tile_logits.reshape(tile_rows, CS + 2, tile_cols, CS + 2, CLASSES)
    glance_logits = jnp.einsum("pi,qj,aibjc->abcpq", table, table, tile_logits, precision=highest)
    glance_logits = glance_logits.reshape(tile_count, CLASSES, TT).astype(jnp.bfloat16)
    rims = jnp.take(jnp.take(bordered, row_index, axis=0), col_index, axis=1)
    rims = rims.reshape(tile_rows, CS + 2, tile_cols, CS + 2, D).transpose(0, 2, 1, 3, 4)
    rims = rims.reshape(tile_count, CS + 2, CS + 2, D)
    flags = unsure.reshape(-1)
    flat_pixels = pixels.reshape(tile_count, TT, PD)
    positions = jnp.arange(tile_count, dtype=jnp.int32)
    capacity = max(2, (UNSURE_MOST + wide_len - 1) // wide_len)
    slot_total = wide_len * capacity
    local_count = jnp.sum(flags)
    before = carried_in(local_count, "wide", add_counts, jnp.zeros((), jnp.int32))
    order = jnp.cumsum(flags) - flags
    target = (before + order) % wide_len
    same = (
        (target[:, None] == target[None, :])
        & (positions[None, :] < positions[:, None])
        & (flags[None, :] == 1)
    )
    depth = jnp.sum(same.astype(jnp.int32), axis=1)
    slot = target * capacity + depth
    slot_ids = jnp.arange(slot_total, dtype=jnp.int32)
    choose = ((flags[None, :] == 1) & (slot[None, :] == slot_ids[:, None])).astype(jnp.int32)
    source = jnp.sum(choose * positions[None, :], axis=1)
    filled = jnp.sum(choose, axis=1)
    send_pixels = flat_pixels[source].reshape(wide_len, capacity, TT, PD)
    send_side = rims[source].reshape(wide_len, capacity, CS + 2, CS + 2, D)
    send_fill = filled.astype(jnp.bfloat16).reshape(wide_len, capacity)
    got_pixels, got_side, got_fill = (
        lax.all_to_all(send_pixels, "wide", split_axis=0, concat_axis=0, tiled=True),
        lax.all_to_all(send_side, "wide", split_axis=0, concat_axis=0, tiled=True),
        lax.all_to_all(send_fill, "wide", split_axis=0, concat_axis=0, tiled=True),
    )
    present = got_fill.reshape(-1).astype(jnp.int32)
    place = jnp.cumsum(present) - present
    pick = (present[None, :] == 1) & (place[None, :] == jnp.arange(RECV, dtype=jnp.int32)[:, None])
    where_from = jnp.sum(pick.astype(jnp.int32) * slot_ids[None, :], axis=1)
    work_pixels = got_pixels.reshape(slot_total, TT, PD)[where_from]
    work_side = got_side.reshape((slot_total,) + got_side.shape[2:])[where_from]
    lifted = jnp.einsum(
        "pi,qj,nijd->npqd", table, table, work_side.astype(jnp.float32), precision=highest
    )
    lifted = lifted.astype(jnp.bfloat16).reshape(work_side.shape[0], TT, D)
    focus_embed = jnp.dot(
        work_pixels.reshape(-1, PD), patch_weight, preferred_element_type=jnp.float32
    )
    focus_embed = focus_embed + jnp.dot(
        lifted.reshape(-1, D), join_weight, preferred_element_type=jnp.float32
    )
    focus_embed = focus_embed.reshape(-1, TT, D) + position.astype(jnp.float32)
    result = attend(focus_embed, gain_attn, qkv_weight, out_weight)
    normed = layer_norm(result, gain_head).astype(jnp.bfloat16).reshape(-1, D)
    answer = jnp.dot(normed, head_weight, preferred_element_type=jnp.float32).reshape(
        -1, TT, CLASSES
    )
    answer = answer.transpose(0, 2, 1).astype(jnp.bfloat16)
    back = jnp.einsum(
        "rs,rck->sck", pick.astype(jnp.bfloat16), answer, preferred_element_type=jnp.float32
    ).astype(jnp.bfloat16)
    returned = lax.all_to_all(
        back.reshape(wide_len, capacity, CLASSES, TT),
        "wide",
        split_axis=0,
        concat_axis=0,
        tiled=True,
    )
    returned = returned.reshape(slot_total, CLASSES, TT)
    focused = returned[jnp.clip(slot, 0, slot_total - 1)]
    result = jnp.where(flags[:, None, None] == 1, focused, glance_logits)
    return result.reshape(tile_rows, tile_cols, CLASSES, TT)


def solution(mesh):
    return jax.shard_map(
        per_device,
        mesh=mesh,
        in_specs=(
            P("wide", "narrow", None, None),
            P("wide", "narrow", None),
            P("wide", "narrow"),
            P(),
            P(),
            P(),
            P(),
            P(),
            P(),
            P(),
            P(),
        ),
        out_specs=P("wide", "narrow", None, None),
        check_vma=False,
    )
```

profile of v0, /device:TPU:0, one launch (start us, length us, event | category | flops | bytes accessed | tf_op | source)
XLA Modules:
  0.0 537.4 jit_solution(16251335013055482713)
XLA Ops:
  5.0 2.2 copy-done.26
  7.2 4.9 convolution_convert_fusion.3
  12.1 4.7 copy.118
  16.8 72.5 %while.38 = (s32[]{:T(128)}, bf16[16,2,256,64]{2,3,0,1:T(8,128)(2,1)}, s32[16]{0:T(128)S(1)}, bf16[2,256,3072]{1,2,0:T(8,128)(2,1)}, s32[]{:T(128)}, /*index=5*/...) while((s32[]{:T(128)}, ...), condition=%wide.region_14.15_spmd, body=%wide.region_11.14_spmd.sunk | while | flops 51282952 | bytes 398111 | solution.py:86
  32.8 2.1 fusion.203
  41.9 2.1 fusion.203
  51.0 2.1 fusion.203
  82.7 2.1 fusion.203
  89.3 3.2 add_convert_fusion
  93.5 2.4 collective-permute-start
  99.9 11.6 %all-reduce = s32[8]{0:T(128)S(1)} all-reduce(s32[8]{0:T(128)S(1)} %dynamic-update-slice), channel_id=1, replica_groups=mesh['wide'=8,'narrow'=4] {'wide'}, use_global_device_ids=true, to_apply=%add | all-reduce | flops 8 | bytes 64
  111.5 9.3 %while.37 = (s32[]{:T(128)}, s32[]{:T(128)}, s32[]{:T(128)}, s32[8]{0:T(128)S(1)}, s32[]{:T(128)}) while((s32[]{:T(128)}, s32[]{:T(128)}, s32[]{:T(128)}, s32[8]{0:T(128)S(1)}, s32[]{:T(128)}) %tuple.90), condition=%wide.region_2.3_spmd, body=%wide.region_1.2_spmd.sunk | while | flops 5 | bytes 107 | solution.py:48
  122.0 3.3 all-to-all-start
  125.3 2.4 copy.121
  131.4 3.5 collective-permute-start.2
  137.3 3.8 collective-permute-done.3
  146.0 3.4 gather_fusion.2
  151.2 2.2 copy.122
  153.4 3.6 gather_fusion.3
  157.1 4.4 copy.123
  161.5 5.0 gather.41
  166.5 2.3 select_bitcast_fusion
  170.1 3.0 copy.125
  173.1 4.3 gather_fusion.4
  177.4 5.6 %copy.126 = bf16[8,4,6,6,1024]{4,1,3,2,0:T(4,128)(2,1)} copy(bf16[8,4,6,6,1024]{4,3,2,1,0:T(8,128)(2,1)} %bitcast.146) | data formatting | bytes 4718592 | tf_op jit(solution)/shard_map/reshape | solution.py:182
  183.0 4.5 all-to-all-start.2
  187.6 11.0 %gather_fusion = bf16[32,256,768]{2,1,0:T(8,128)(2,1)} fusion(bf16[32,256,768]{2,1,0:T(8,128)(2,1)} %bitcast.147, s32[1024]{0:T(1024)S(1)} %pad_clamp_fusion.4), kind=kCustom, calls=%fused_computation | custom fusion | bytes 25165952 | tf_op jit(solution)/shard_map/gather | solution.py:181
  198.6 18.4 %all-to-all-done.2 = bf16[8,4,6,6,1024]{4,1,3,2,0:T(4,128)(2,1)} async-done(((bf16[8,4,6,6,1024]{4,1,3,2,0:T(4,128)(2,1)}), bf16[8,4,6,6,1024]{4,1,3,2,0:T(4,128)(2,1)}, u32[]{:S(2)}, u32[]{:S(2)}) %all-to-all-start.2) | async-done | bytes 2359328 | tf_op jit(solution)/shard_map/all_to_all | solution.py:186
  217.1 5.5 %all-to-all-start.1 = ((bf16[8,4,256,768]{3,2,1,0:T(8,128)(2,1)}), bf16[8,4,256,768]{3,2,1,0:T(8,128)(2,1)}, u32[]{:S(2)}, u32[]{:S(2)}) async-start(bf16[8,4,256,768]{3,2,1,0:T(8,128)(2,1)} %bitcast.140), calls=%async_computation.1 | async-start | bytes 25165824 | tf_op jit(solution)/shard_map/all_to_all | solution.py:185
  227.4 2.4 fusion.101
  234.7 2.1 copy.139
  240.1 3.9 fusion.105
  244.1 4.2 copy.127
  248.3 3.3 gather_fusion.5
  251.6 2.8 fusion.107
  254.4 8.7 %fusion.86 = bf16[7,1024,16,16]{1,3,2,0:T(8,128)(2,1)} fusion(f32[7,6,1024,16]{2,3,1,0:T(8,128)S(1)} %fusion.107, f32[16]{0:T(128)S(1)} %get-tuple-element.275, s32[16]{0:T(128)S(1)} %copy-done.11, f32[16]{0:T(128)S(1)} %get-tuple-element.276, s32[16]{0:T(128)S(1)} %get-tuple-element.277), kind=kOutput, calls=%fused_computation.68 | convolution fusion | flops 133956064 | bytes 6422784 | tf_op jit(solution)/shard_map/pi,qj,nijd->npqd/dot_general | solution.py:195
  263.2 98.5 %all-to-all-done.1 = bf16[8,4,256,768]{3,2,1,0:T(8,128)(2,1)} async-done(((bf16[8,4,256,768]{3,2,1,0:T(8,128)(2,1)}), bf16[8,4,256,768]{3,2,1,0:T(8,128)(2,1)}, u32[]{:S(2)}, u32[]{:S(2)}) %all-to-all-start.1) | async-done | bytes 12582944 | tf_op jit(solution)/shard_map/all_to_all | solution.py:185
  361.6 6.9 %gather_fusion.1 = bf16[7,256,768]{2,1,0:T(8,128)(2,1)} fusion(bf16[32,256,768]{2,1,0:T(8,128)(2,1)} %bitcast.11, s32[1024]{0:T(1024)S(1)} %pad_clamp_fusion.3), kind=kCustom, calls=%fused_computation.1 | custom fusion | bytes 5505052 | tf_op jit(solution)/shard_map/gather | solution.py:193
  368.5 5.5 %fusion.170 = f32[1792,1024]{1,0:T(8,128)S(1)} fusion(bf16[1792,768]{1,0:T(8,128)(2,1)} %bitcast.154, bf16[768,1024]{1,0:T(8,128)(2,1)} %param.20), kind=kOutput, calls=%fused_computation.212 | convolution fusion | flops 2818572288 | bytes 11665408 | tf_op jit(solution)/shard_map/dot_general | solution.py:199
  374.0 4.9 fusion.77
  380.2 2.3 copy-done.1
  384.6 14.5 %convolution_convert_fusion.2 = bf16[1792,3072]{1,0:T(8,128)(2,1)} fusion(bf16[1792,1024]{1,0:T(8,128)(2,1)S(1)} %multiply_convert_fusion.1, bf16[1024,3072]{1,0:T(8,128)(2,1)S(1)} %bitcast.168), kind=kOutput, calls=%fused_computation.46 | convolution fusion | flops 11279794176 | bytes 20971520 | tf_op jit(solution)/shard_map/dot_general | solution.py:71
  399.1 14.6 %copy.130 = bf16[7,256,3072]{1,2,0:T(8,128)(2,1)} copy(bf16[7,256,3072]{2,1,0:T(8,128)(2,1)} %bitcast.148) | data formatting | bytes 22020096 | tf_op jit(solution)/shard_map/while | solution.py:86
  413.7 93.4 %while.39 = (s32[]{:T(128)}, bf16[16,7,256,64]{2,3,0,1:T(8,128)(2,1)}, s32[16]{0:T(128)S(1)}, bf16[7,256,3072]{1,2,0:T(8,128)(2,1)}, s32[]{:T(128)}, /*index=5*/...) while((s32[]{:T(128)}, ...), condition=%wide.region_20.21_spmd, body=%wide.region_17.20_spmd.sunk | while | flops 179489024 | bytes 1391391 | solution.py:86
  416.8 2.8 fusion.211
  422.6 2.8 fusion.211
  428.5 2.8 fusion.211
  434.3 2.8 fusion.211
  440.1 2.8 fusion.211
  446.0 2.8 fusion.211
  451.8 2.8 fusion.211
  457.6 2.8 fusion.211
  463.5 2.8 fusion.211
  469.3 2.8 fusion.211
  475.1 2.8 fusion.211
  481.0 2.8 fusion.211
  486.8 2.8 fusion.211
  492.7 2.8 fusion.211
  498.5 2.8 fusion.211
  504.4 2.8 fusion.211
  507.1 8.8 %fusion.169 = (f32[7,256]{1,0:T(8,128)S(1)}, f32[7,256,1024]{2,1,0:T(8,128)S(1)}) fusion(bf16[7,256,1024]{1,2,0:T(8,128)(2,1)} %bitcast.169, bf16[1024,1024]{1,0:T(8,128)(2,1)S(1)} %copy-done, f32[7,256,1024]{2,1,0:T(8,128)} %bitcast.139, f32[256,1024]{1,0:T(8,128)S(1)} %convert_element_type.155), kind=kOutput, calls=%fused_computation.211 | convolution fusion | flops 3763599616 | bytes 21502976 | tf_op jit(solution)/shard_map/dot_general | solution.py:88
  519.6 3.6 all-to-all-start.3
  523.2 9.3 %fusion.94 = bf16[4,8,16,16,16]{4,3,2,1,0:T(8,128)(2,1)} fusion(f32[4,8,6,16,16]{4,3,2,1,0:T(8,128)} %fusion.105, f32[16]{0:T(128)S(1)} %get-tuple-element.275, s32[16]{0:T(128)S(1)} %copy-done.11, f32[16]{0:T(128)S(1)} %get-tuple-element.276, s32[16]{0:T(128)S(1)} %get-tuple-element.277), kind=kOutput, calls=%fused_computation.79 | convolution fusion | flops 9568736 | bytes 459008 | tf_op jit(solution)/shard_map/pi,qj,aibjc->abcpq/dot_general | solution.py:156
  532.5 3.2 convert_element_type.171
  (244 shorter events, 143.9 us)
Async XLA Ops:
  0.0 89.3 %copy-start = (bf16[1024,1024]{1,0:T(8,128)(2,1)S(1)}, bf16[1024,1024]{1,0:T(8,128)(2,1)}, u32[]{:S(2)}) copy-start(bf16[1024,1024]{1,0:T(8,128)(2,1)} %param.23) | copy-start | bytes 6291460
  0.0 2.5 copy-start.6
  3.6 1.4 copy-start.3
  3.6 0.7 copy-start.10
  3.6 3.5 copy-start.26
  89.3 7.9 %copy-start.9 = (s32[4,8]{1,0:T(4,128)S(1)}, s32[4,8]{1,0:T(4,128)}, u32[]{:S(2)}) copy-start(s32[4,8]{1,0:T(4,128)} %param.19) | copy-start | bytes 388
  89.3 8.7 %copy-start.27 = (u32[32]{0:T(128)S(1)}, u32[32]{0:T(128)}, u32[]{:S(2)}) copy-start(u32[32]{0:T(128)} %constant.297) | copy-start | bytes 388
  92.5 1.0 copy-start.7
  93.5 36.1 %collective-permute-start = (bf16[1,32,1024]{2,1,0:T(8,128)(2,1)S(1)}, bf16[1,32,1024]{2,1,0:T(8,128)(2,1)S(1)}, u32[]{:S(2)}, u32[]{:S(2)}) collective-permute-start(bf16[1,32,1024]{2,1,0:T(8,128)(2,1)S(1)} %bitcast.163), channel_id=1, source_target_pairs={{0,4},{4,8},{8,12},{12,16},{16,20},{20,24},{24,28},{1,5},{5,9},{9,... | collective-permute-start | bytes 196616 | tf_op jit(solution)/shard_map/ppermute | solution.py:29
  95.9 33.7 %collective-permute-start.1 = (bf16[1,32,1024]{2,1,0:T(8,128)(2,1)S(1)}, bf16[1,32,1024]{2,1,0:T(8,128)(2,1)S(1)}, u32[]{:S(2)}, u32[]{:S(2)}) collective-permute-start(bf16[1,32,1024]{2,1,0:T(8,128)(2,1)S(1)} %bitcast.162), channel_id=1, source_target_pairs={{4,0},{8,4},{12,8},{16,12},{20,16},{24,20},{28,24},{5,1},{9,5},{13... | collective-permute-start | bytes 196616 | tf_op jit(solution)/shard_map/ppermute | solution.py:31
  121.2 8.1 %copy-start.19 = (s32[32]{0:T(128)}, s32[32]{0:T(128)S(1)}, u32[]{:S(2)}) copy-start(s32[32]{0:T(128)S(1)} %convert_reduce_fusion.2) | copy-start | bytes 388
  122.0 61.0 %all-to-all-start = ((bf16[8,1,4]{2,1,0:T(2,128)(2,1)}), bf16[8,1,4]{2,1,0:T(2,128)(2,1)S(1)}, u32[]{:S(2)}, u32[]{:S(2)}) async-start(bf16[8,1,4]{2,1,0:T(2,128)(2,1)} %convert_element_type.174), calls=%async_computation | async-start | bytes 8192 | tf_op jit(solution)/shard_map/all_to_all | solution.py:187
  128.7 17.4 %copy-start.12 = (s32[1024]{0:T(1024)}, s32[1024]{0:T(1024)S(1)}, u32[]{:S(2)}) copy-start(s32[1024]{0:T(1024)S(1)} %pad_clamp_fusion.2) | copy-start | bytes 12292
  129.6 23.9 %copy-start.13 = (s32[1024]{0:T(1024)}, s32[1024]{0:T(1024)S(1)}, u32[]{:S(2)}) copy-start(s32[1024]{0:T(1024)S(1)} %pad_clamp_fusion.1) | copy-start | bytes 12292
  131.4 5.9 %collective-permute-start.2 = (bf16[18,1,1024]{2,1,0:T(2,128)(2,1)}, bf16[18,1,1024]{2,1,0:T(2,128)(2,1)S(1)}, u32[]{:S(2)}, u32[]{:S(2)}) collective-permute-start(bf16[18,1,1024]{2,1,0:T(2,128)(2,1)} %get-tuple-element.265), channel_id=1, source_target_pairs={{0,1},{1,2},{2,3},{4,5},{5,6},{6,7},{8,9},{9,10},{10,11},{12,13},{... | collective-permute-start | bytes 110600 | tf_op jit(solution)/shard_map/ppermute | solution.py:29
  134.8 6.2 %collective-permute-start.3 = (bf16[18,1,1024]{2,1,0:T(2,128)(2,1)S(1)}, bf16[18,1,1024]{2,1,0:T(2,128)(2,1)S(1)}, u32[]{:S(2)}, u32[]{:S(2)}) collective-permute-start(bf16[18,1,1024]{2,1,0:T(2,128)(2,1)S(1)} %get-tuple-element.266), channel_id=1, source_target_pairs={{1,0},{2,1},{3,2},{5,4},{6,5},{7,6},{9,8},{10,9},{11,10},{13,12},{... | collective-permute-start | bytes 110600 | tf_op jit(solution)/shard_map/ppermute | solution.py:31
  136.7 6.5 %copy-start.2 = (bf16[1,16,2,16,1024]{4,3,2,1,0:T(8,128)(2,1)S(1)}, bf16[1,16,2,16,1024]{4,3,2,1,0:T(8,128)(2,1)}, u32[]{:S(2)}) copy-start(bf16[1,16,2,16,1024]{4,3,2,1,0:T(8,128)(2,1)} %copy.121) | copy-start | bytes 3145732
  144.3 5.2 copy-start.18
  161.5 5.0 copy-start.16
  183.0 34.0 %all-to-all-start.2 = ((bf16[8,4,6,6,1024]{4,1,3,2,0:T(4,128)(2,1)}), bf16[8,4,6,6,1024]{4,1,3,2,0:T(4,128)(2,1)}, u32[]{:S(2)}, u32[]{:S(2)}) async-start(bf16[8,4,6,6,1024]{4,1,3,2,0:T(4,128)(2,1)} %copy.126), calls=%async_computation.2 | async-start | bytes 4718592 | tf_op jit(solution)/shard_map/all_to_all | solution.py:186
  217.1 5.6 %copy-start.20 = (s32[32]{0:T(128)S(1)}, s32[32]{0:T(128)}, u32[]{:S(2)}) copy-start(s32[32]{0:T(128)} %copy-done.19) | copy-start | bytes 388
  217.1 10.3 %copy-start.8 = (bf16[1024,16]{0,1:T(8,128)(2,1)S(1)}, bf16[1024,16]{0,1:T(8,128)(2,1)}, u32[]{:S(2)}) copy-start(bf16[1024,16]{0,1:T(8,128)(2,1)} %param.27) | copy-start | bytes 98308
  217.1 10.3 %copy-start.14 = (f32[1024]{0:T(1024)S(1)}, f32[1024]{0:T(1024)}, u32[]{:S(2)}) copy-start(f32[1024]{0:T(1024)} %param.26) | copy-start | bytes 12292
  217.1 144.5 %all-to-all-start.1 = ((bf16[8,4,256,768]{3,2,1,0:T(8,128)(2,1)}), bf16[8,4,256,768]{3,2,1,0:T(8,128)(2,1)}, u32[]{:S(2)}, u32[]{:S(2)}) async-start(bf16[8,4,256,768]{3,2,1,0:T(8,128)(2,1)} %bitcast.140), calls=%async_computation.1 | async-start | bytes 25165824 | tf_op jit(solution)/shard_map/all_to_all | solution.py:185
  224.8 0.5 copy-start.22
  224.9 0.6 copy-start.24
  229.8 9.1 %copy-start.17 = (pred[8,6]{1,0:T(8,128)(4,1)S(1)}, pred[8,6]{1,0:T(8,128)(4,1)}, u32[]{:S(2)}) copy-start(pred[8,6]{1,0:T(8,128)(4,1)} %compare_and_fusion) | copy-start | bytes 148
  230.6 9.5 %copy-start.11 = (s32[16]{0:T(128)S(1)}, s32[16]{0:T(128)}, u32[]{:S(2)}) copy-start(s32[16]{0:T(128)} %get-tuple-element.278) | copy-start | bytes 196
  368.5 5.5 %copy-start.4 = (bf16[7,1024,16,16]{1,3,2,0:T(8,128)(2,1)S(1)}, bf16[7,1024,16,16]{1,3,2,0:T(8,128)(2,1)}, u32[]{:S(2)}) copy-start(bf16[7,1024,16,16]{1,3,2,0:T(8,128)(2,1)} %fusion.86) | copy-start | bytes 11010052
  368.5 5.5 %copy-start.5 = (bf16[1024,1024]{1,0:T(8,128)(2,1)S(1)}, bf16[1024,1024]{1,0:T(8,128)(2,1)}, u32[]{:S(2)}) copy-start(bf16[1024,1024]{1,0:T(8,128)(2,1)} %param.24) | copy-start | bytes 6291460
  378.8 3.7 copy-start.1
  378.9 5.0 slice-start
  382.6 2.0 slice-start.1
  516.0 0.9 copy-start.15
  516.9 1.5 copy-start.23
  516.9 1.5 copy-start.25
  519.6 16.1 %all-to-all-start.3 = ((bf16[8,4,16,256]{3,1,2,0:T(4,128)(2,1)}), bf16[8,4,16,256]{3,1,2,0:T(4,128)(2,1)S(1)}, u32[]{:S(2)}, u32[]{:S(2)}) async-start(bf16[8,4,16,256]{3,1,2,0:T(4,128)(2,1)} %copy.134), calls=%async_computation.3 | async-start | bytes 524288 | tf_op jit(solution)/shard_map/all_to_all | solution.py:215
  523.2 13.2 %copy-start.21 = (pred[4,8]{1,0:T(4,128)(4,1)S(1)}, pred[4,8]{1,0:T(4,128)(4,1)}, u32[]{:S(2)}) copy-start(pred[4,8]{1,0:T(4,128)(4,1)} %broadcast_compare_fusion) | copy-start | bytes 100
where the time goes:
time: 547 us; the launch traced here: 537 us
  matrix products  199 us (36%)
  local copies, waits for them, and re-layouts  128 us (23%)
  waiting for transfers between devices  121 us (22%)
  other arithmetic  26.2 us (5%)
  starting transfers between devices  25.9 us (5%)
  loops' own time  25 us (5%)
  blocking collectives  11.6 us (2%)
    all_to_all x1, waiting for transfers between devices, per_device(): lax.all_to_all(send_pixels, 'wide', split_axis=0, concat_axis=0, tiled=True)  98.5 us
    dot_general x32, matrix products, one_head(): jnp.einsum('nqk,nkd->nqd', weights, value_rows, preferred_element_type=jn...  77.6 us
    sub x32, matrix products, one_head(): weights = jax.nn.softmax(scores, axis=-1).astype(jnp.bfloat16)  49.2 us
    another operation x2, loops' own time, attend(): heads_out = lax.map(one_head, jnp.arange(HEADS, dtype=jnp.int32))  20.4 us
    dot_general x2, matrix products, attend(): jnp.dot(normed, qkv_weight, preferred_element_type=jnp.float32)  19.4 us
    while x2, local copies, waits for them, and re-layouts, attend(): heads_out = lax.map(one_head, jnp.arange(HEADS, dtype=jnp.int32))  19.3 us
    dynamic_slice x32, local copies, waits for them, and re-layouts, attend(): heads_out = lax.map(one_head, jnp.arange(HEADS, dtype=jnp.int32))  18.7 us
    all_to_all x1, waiting for transfers between devices, per_device(): lax.all_to_all(send_side, 'wide', split_axis=0, concat_axis=0, tiled=True)  18.4 us
  transfers between devices with their start and end apart: 8, of which 4 were waited for; matrix products, arithmetic and copies ran while one was open for 22% of the time, Pallas kernels for 0%

commit v1 on v0

v1 whole, which is shorter than its diff:
```python
import functools

import jax
import jax.numpy as jnp
from jax import lax
from jax.experimental import pallas as pl
from jax.experimental.pallas import tpu as pltpu
from jax.sharding import PartitionSpec as P

D = 1024
HEADS = 16
HD = 64
PD = 768
CLASSES = 16
TS = 16
TT = 256
CS = 4
UNSURE_MOST = 25
RECV = 7


EPS = 1e-06


def padded(cells, sides, width):
    for axis, dim in sides:
        count = lax.axis_size(axis)
        ends = count - 1
        head = lax.slice_in_dim(cells, 0, width, axis=dim)
        tail = lax.slice_in_dim(cells, cells.shape[dim] - width, cells.shape[dim], axis=dim)
        cells = jnp.concatenate(
            [
                lax.ppermute(tail, axis, [(i, (i + 1) % count) for i in range(ends)]),
                cells,
                lax.ppermute(head, axis, [((i + 1) % count, i) for i in range(ends)]),
            ],
            axis=dim,
        )
    return cells


def carried_in(x, axis, combine, identity):
    count, position = (lax.axis_size(axis), lax.axis_index(axis))
    everything = lax.all_gather(x, axis)
    start = jnp.broadcast_to(jnp.asarray(identity, x.dtype), x.shape)

    def step(k, before):
        reached = k < position
        new = combine(before, everything[k])
        return jnp.where(reached, new, before)

    return lax.fori_loop(0, count, step, start)


def interp_table():
    fine = jnp.arange(TS, dtype=jnp.int32)
    eighths = 2 * fine - 3
    lower = eighths // 8
    frac = (eighths - 8 * lower).astype(jnp.float32) / 8.0
    column = jnp.arange(CS + 2, dtype=jnp.int32)
    left = (column[None, :] == (lower + 1)[:, None]).astype(jnp.float32)
    right = (column[None, :] == (lower + 2)[:, None]).astype(jnp.float32)
    return left * (1.0 - frac)[:, None] + right * frac[:, None]


def layer_norm(values, gain):
    center = values - jnp.mean(values, axis=-1, keepdims=True)
    spread = jnp.mean(center * center, axis=-1, keepdims=True)
    return center * lax.rsqrt(spread + EPS) * gain


RIM = 48
RIM_USED = (CS + 2) * (CS + 2)
LOG2E = 1.4426950408889634
VMEM_BYTES = 56 * 1024 * 1024


def dot(a, b):
    return jnp.dot(a, b, preferred_element_type=jnp.float32)


def dot_t(a, b):
    return lax.dot_general(a, b, (((1,), (1,)), ((), ())), preferred_element_type=jnp.float32)


def attend_tile(tokens, gain_ref, qkv_ref, out_ref, mixed_ref):
    normed = layer_norm(tokens, gain_ref[...]).astype(jnp.bfloat16)
    lane = lax.broadcasted_iota(jnp.int32, (TT, 2 * HD), 1)
    first = lane < HD
    ones_a = jnp.where(first, 1.0, 0.0).astype(jnp.bfloat16)
    ones_b = jnp.where(first, 0.0, 1.0).astype(jnp.bfloat16)
    zero = jnp.zeros((TT, 2 * HD), jnp.bfloat16)
    wide = 4 * HD
    for group in range(D // wide):
        at = group * wide
        q = dot(normed, qkv_ref[:, at : at + wide]).astype(jnp.bfloat16)
        k = dot(normed, qkv_ref[:, D + at : D + at + wide]).astype(jnp.bfloat16)
        v = dot(normed, qkv_ref[:, 2 * D + at : 2 * D + at + wide]).astype(jnp.bfloat16)
        for pair in range(2):
            cols = slice(pair * 2 * HD, (pair + 1) * 2 * HD)
            q2, k2, v2 = q[:, cols], k[:, cols], v[:, cols]
            parts = []
            for mine in (first, ~first):
                s = dot_t(jnp.where(mine, q2, zero), k2)
                top = jnp.max(s, axis=-1, keepdims=True)
                parts.append(jnp.exp2((s - top) * (LOG2E * HD ** (-0.5))).astype(jnp.bfloat16))
            p = jnp.concatenate(parts, axis=1)
            upper = jnp.concatenate([jnp.where(first, v2, zero), ones_a], axis=1)
            lower = jnp.concatenate([jnp.where(first, zero, v2), ones_b], axis=1)
            o = dot(p, jnp.concatenate([upper, lower], axis=0))
            mixed_ref[:, at + pair * 2 * HD : at + (pair + 1) * 2 * HD] = (
                o[:, : 2 * HD] / o[:, 2 * HD :]
            ).astype(jnp.bfloat16)
    return tokens + dot(mixed_ref[...], out_ref[...])


def glance_kernel(px_ref, patch_ref, pos_ref, gain_ref, qkv_ref, out_ref, feat_ref, mixed_ref):
    patches = px_ref[...].reshape(TT, PD)
    embed = dot(patches, patch_ref[...]) + pos_ref[...].astype(jnp.float32)
    result = attend_tile(embed, gain_ref, qkv_ref, out_ref, mixed_ref)
    feat_ref[...] = result.astype(jnp.bfloat16).reshape(feat_ref.shape)


def fixed(shape):
    return pl.BlockSpec(
        shape, lambda *_: (0,) * len(shape), pipeline_mode=pl.Buffered(1)
    )


def glance(coarse, patch_weight, position, gain_attn, qkv_weight, out_weight):
    rows, cols, _ = coarse.shape
    count = (rows // TS) * (cols // TS)
    return pl.pallas_call(
        glance_kernel,
        grid=(rows // TS, cols // TS),
        in_specs=[
            pl.BlockSpec((TS, TS, PD), lambda a, b: (a, b, 0)),
            fixed((PD, D)),
            fixed((TT, D)),
            fixed((1, D)),
            fixed((D, 3 * D)),
            fixed((D, D)),
        ],
        out_specs=pl.BlockSpec((TS, TS, D), lambda a, b: (a, b, 0)),
        out_shape=jax.ShapeDtypeStruct((rows, cols, D), jnp.bfloat16),
        scratch_shapes=[pltpu.VMEM((TT, D), jnp.bfloat16)],
        compiler_params=pltpu.CompilerParams(vmem_limit_bytes=VMEM_BYTES),
        cost_estimate=pl.CostEstimate(
            flops=count * 4_000_000_000, bytes_accessed=14_000_000, transcendentals=0
        ),
    )(coarse, patch_weight, position, gain_attn.reshape(1, D), qkv_weight, out_weight)


def focus_kernel(
    where_ref,
    px_ref,
    rim_ref,
    lift_ref,
    patch_ref,
    join_ref,
    pos_ref,
    gain_ref,
    qkv_ref,
    out_ref,
    gain_head_ref,
    head_ref,
    answer_ref,
    mixed_ref,
):
    joined = dot(rim_ref[0], join_ref[...])
    high = joined.astype(jnp.bfloat16)
    low = (joined - high.astype(jnp.float32)).astype(jnp.bfloat16)
    embed = dot(px_ref[0], patch_ref[...])
    embed = embed + dot(lift_ref[...], jnp.concatenate([high, low], axis=0))
    embed = embed + pos_ref[...].astype(jnp.float32)
    result = attend_tile(embed, gain_ref, qkv_ref, out_ref, mixed_ref)
    normed = layer_norm(result, gain_head_ref[...]).astype(jnp.bfloat16)
    answer_ref[0] = dot_t(head_ref[...], normed).astype(jnp.bfloat16)


def focus(where_from, pixels, rims, lift, weights):
    patch_weight, join_weight, position, gain_attn, qkv_weight, out_weight, gain_head, head_t = weights
    count = where_from.shape[0]
    return pl.pallas_call(
        focus_kernel,
        grid_spec=pltpu.PrefetchScalarGridSpec(
            num_scalar_prefetch=1,
            grid=(count,),
            in_specs=[
                pl.BlockSpec((1, TT, PD), lambda i, w: (w[i], 0, 0)),
                pl.BlockSpec((1, RIM, D), lambda i, w: (w[i], 0, 0)),
                fixed((TT, 2 * RIM)),
                fixed((PD, D)),
                fixed((D, D)),
                fixed((TT, D)),
                fixed((1, D)),
                fixed((D, 3 * D)),
                fixed((D, D)),
                fixed((1, D)),
                fixed((CLASSES, D)),
            ],
            out_specs=pl.BlockSpec((1, CLASSES, TT), lambda i, w: (i, 0, 0)),
            scratch_shapes=[pltpu.VMEM((TT, D), jnp.bfloat16)],
        ),
        out_shape=jax.ShapeDtypeStruct((count, CLASSES, TT), jnp.bfloat16),
        compiler_params=pltpu.CompilerParams(vmem_limit_bytes=VMEM_BYTES),
        cost_estimate=pl.CostEstimate(
            flops=count * 4_500_000_000, bytes_accessed=20_000_000, transcendentals=0
        ),
    )(
        where_from,
        pixels,
        rims,
        lift,
        patch_weight,
        join_weight,
        position,
        gain_attn.reshape(1, D),
        qkv_weight,
        out_weight,
        gain_head.reshape(1, D),
        head_t,
    )


def lift_table():
    table = interp_table()
    both = (table[:, None, :, None] * table[None, :, None, :]).reshape(TT, RIM_USED)
    return jnp.pad(both, ((0, 0), (0, RIM - RIM_USED))).astype(jnp.bfloat16)


def rim_cells(tiles, tile_cols, cols):
    k = jnp.arange(RIM, dtype=jnp.int32)
    cell = (tiles // tile_cols * CS)[:, None] + k[None, :] // (CS + 2)
    cell = cell * cols + (tiles % tile_cols * CS)[:, None] + k[None, :] % (CS + 2)
    return jnp.where(k[None, :] < RIM_USED, cell, -1)


def bordered_features(features):
    bordered = padded(features, (("wide", 0), ("narrow", 1)), 1)
    wide_pos = lax.axis_index("wide")
    narrow_pos = lax.axis_index("narrow")
    top_row = jnp.where(wide_pos == 0, bordered[1:2], bordered[0:1])
    bottom_row = jnp.where(
        wide_pos == lax.axis_size("wide") - 1, bordered[-2:-1], bordered[-1:]
    )
    bordered = jnp.concatenate([top_row, bordered[1:-1], bottom_row], axis=0)
    left_col = jnp.where(narrow_pos == 0, bordered[:, 1:2], bordered[:, 0:1])
    right_col = jnp.where(
        narrow_pos == lax.axis_size("narrow") - 1, bordered[:, -2:-1], bordered[:, -1:]
    )
    bordered = jnp.concatenate([left_col, bordered[:, 1:-1], right_col], axis=1)
    return bordered


def glance_answer(flat, gain_head, head_weight, cells, lift):
    tile_count = cells.shape[0]
    normed = layer_norm(flat.astype(jnp.float32), gain_head).astype(jnp.bfloat16)
    coarse = lax.dot_general(
        head_weight, normed, (((0,), (1,)), ((), ())), preferred_element_type=jnp.float32
    )
    pieces = []
    for _ in range(3):
        piece = lax.reduce_precision(coarse, 8, 7)
        pieces.append(piece.astype(jnp.bfloat16))
        coarse = coarse - piece
    stacked = jnp.concatenate(pieces, axis=0)
    chosen = (
        jnp.arange(flat.shape[0], dtype=jnp.int32)[:, None] == cells.reshape(1, -1)
    ).astype(jnp.bfloat16)
    rim_logits = dot(stacked, chosen).astype(jnp.bfloat16).reshape(3 * CLASSES * tile_count, RIM)
    fine = dot_t(rim_logits, lift).reshape(3, CLASSES, tile_count, TT)
    return (fine[0] + fine[1] + fine[2]).astype(jnp.bfloat16).transpose(1, 0, 2)


def per_device(
    pixels,
    coarse_pixels,
    unsure,
    patch_weight,
    position,
    qkv_weight,
    out_weight,
    join_weight,
    gain_attn,
    gain_head,
    head_weight,
):
    tile_rows, tile_cols = unsure.shape
    tile_count = tile_rows * tile_cols
    wide_pos = lax.axis_index("wide")
    wide_len = lax.axis_size("wide")
    flags = unsure.reshape(-1)
    flat_pixels = pixels.reshape(tile_count, TT, PD)
    positions = jnp.arange(tile_count, dtype=jnp.int32)
    capacity = max(2, (UNSURE_MOST + wide_len - 1) // wide_len)
    slot_total = wide_len * capacity
    local_count = jnp.sum(flags)
    before = carried_in(local_count, "wide", jnp.add, jnp.zeros((), jnp.int32))
    order = jnp.cumsum(flags) - flags
    target = (before + order) % wide_len
    same = (
        (target[:, None] == target[None, :])
        & (positions[None, :] < positions[:, None])
        & (flags[None, :] == 1)
    )
    depth = jnp.sum(same.astype(jnp.int32), axis=1)
    slot = target * capacity + depth
    slot_ids = jnp.arange(slot_total, dtype=jnp.int32)
    choose = ((flags[None, :] == 1) & (slot[None, :] == slot_ids[:, None])).astype(jnp.int32)
    source = jnp.sum(choose * positions[None, :], axis=1)
    filled = jnp.sum(choose, axis=1)
    exchange = functools.partial(
        lax.all_to_all, axis_name="wide", split_axis=0, concat_axis=0, tiled=True
    )
    got_pixels = exchange(flat_pixels[source])
    got_fill = exchange(filled.astype(jnp.bfloat16).reshape(wide_len, capacity))
    features = glance(coarse_pixels, patch_weight, position, gain_attn, qkv_weight, out_weight)
    bordered = bordered_features(features)
    cols = bordered.shape[1]
    flat = bordered.reshape(-1, D)
    lift = lift_table()
    cells = rim_cells(positions, tile_cols, cols)
    send_cells = rim_cells(source, tile_cols, cols).reshape(-1)
    chosen = (
        send_cells[:, None] == jnp.arange(flat.shape[0], dtype=jnp.int32)[None, :]
    ).astype(jnp.bfloat16)
    got_side = exchange(dot(chosen, flat).astype(jnp.bfloat16).reshape(slot_total, RIM, D))
    glance_logits = glance_answer(flat, gain_head, head_weight, cells, lift)
    present = got_fill.reshape(-1).astype(jnp.int32)
    place = jnp.cumsum(present) - present
    pick = (present[None, :] == 1) & (place[None, :] == jnp.arange(RECV, dtype=jnp.int32)[:, None])
    where_from = jnp.sum(pick.astype(jnp.int32) * slot_ids[None, :], axis=1)
    weights = (
        patch_weight,
        join_weight,
        position,
        gain_attn,
        qkv_weight,
        out_weight,
        gain_head,
        head_weight.T,
    )
    answer = focus(
        where_from, got_pixels, got_side, jnp.concatenate([lift, lift], axis=1), weights
    )
    back = dot(
        pick.astype(jnp.bfloat16).T, answer.reshape(RECV, CLASSES * TT)
    ).astype(jnp.bfloat16)
    returned = exchange(back.reshape(slot_total, CLASSES, TT))
    focused = returned[jnp.clip(slot, 0, slot_total - 1)]
    result = jnp.where(flags[:, None, None] == 1, focused, glance_logits)
    return result.reshape(tile_rows, tile_cols, CLASSES, TT)


def solution(mesh):
    return jax.shard_map(
        per_device,
        mesh=mesh,
        in_specs=(
            P("wide", "narrow", None, None),
            P("wide", "narrow", None),
            P("wide", "narrow"),
            P(),
            P(),
            P(),
            P(),
            P(),
            P(),
            P(),
            P(),
        ),
        out_specs=P("wide", "narrow", None, None),
        check_vma=False,
    )
```

time: 547 us -> 324 us (0.59); the launches traced: 537 us -> 324 us
  matrix products: 199 us -> 6.43 us
  local copies, waits for them, and re-layouts: 128 us -> 26.4 us
  Pallas kernels: 0 us -> 65.7 us
  waiting for transfers between devices: 121 us -> 170 us
  loops' own time: 25 us -> 5.76 us
  other arithmetic: 26.2 us -> 9.98 us
    dot_general x46 -> x5, matrix products: 149 us -> 6.43 us  [the longest x3 5.37 us: dot(): return jnp.dot(a, b, preferred_element_type=jnp.float32)]
    pallas_call x0 -> x2, Pallas kernels: none -> 65.7 us  [the longest x1 50.1 us: focus(): pl.pallas_call(focus_kernel, grid_spec=pltpu.PrefetchScalarGridSpec(num_s...]
    all_to_all x4, waiting for transfers between devices: 117 us -> 167 us  [the longest x1 133 us: per_device(): got_pixels = exchange(flat_pixels[source])]
    sub x32 -> x0, matrix products: 49.2 us -> none  [one_head(): weights = jax.nn.softmax(scores, axis=-1).astype(jnp.bfloat16)]
    gather x12 -> x1, local copies, waits for them, and re-layouts: 48.4 us -> 10.9 us  [per_device(): got_pixels = exchange(flat_pixels[source])]
    another operation x2 -> x0, loops' own time: 20.4 us -> none  [attend(): heads_out = lax.map(one_head, jnp.arange(HEADS, dtype=jnp.int32))]
    while x2 -> x0, local copies, waits for them, and re-layouts: 19.3 us -> none  [attend(): heads_out = lax.map(one_head, jnp.arange(HEADS, dtype=jnp.int32))]
    dynamic_slice x32 -> x0, local copies, waits for them, and re-layouts: 18.7 us -> none  [attend(): heads_out = lax.map(one_head, jnp.arange(HEADS, dtype=jnp.int32))]
  transfers between devices with their start and end apart: 8 -> 8, of which waited for: 4 -> 6; matrix products, arithmetic and copies ran while one was open for 22% -> 8% of each run, Pallas kernels for 0% -> 5%
where the time goes in v1:
time: 324 us
  waiting for transfers between devices  170 us (52%)
  Pallas kernels  65.7 us (20%)
  starting transfers between devices  30 us (9%)
  local copies, waits for them, and re-layouts  26.4 us (8%)
  other arithmetic  9.98 us (3%)
  blocking collectives  9.46 us (3%)
  matrix products  6.43 us (2%)
  loops' own time  5.76 us (2%)
    all_to_all x1, waiting for transfers between devices, per_device(): got_pixels = exchange(flat_pixels[source])  133 us
    pallas_call x1, Pallas kernels, focus(): pl.pallas_call(focus_kernel, grid_spec=pltpu.PrefetchScalarGridSpec(num_s...  50.1 us
    all_to_all x1, waiting for transfers between devices, per_device(): exchange(dot(chosen, flat).astype(jnp.bfloat16).reshape(slot_total, RIM, D))  26.8 us
    pallas_call x1, Pallas kernels, glance(): pl.pallas_call(glance_kernel, grid=(rows // TS, cols // TS), in_specs=[pl...  15.6 us
    gather x1, local copies, waits for them, and re-layouts, per_device(): got_pixels = exchange(flat_pixels[source])  10.9 us
    unnamed x1, blocking collectives  9.46 us
    ppermute x2, starting transfers between devices, padded(): lax.ppermute(tail, axis, [(i, (i + 1) % count) for i in range(ends)])  7.58 us
    all_to_all x1, starting transfers between devices, per_device(): exchange(dot(chosen, flat).astype(jnp.bfloat16).reshape(slot_total, RIM, D))  7.57 us
  transfers between devices with their start and end apart: 8, of which 6 were waited for; matrix products, arithmetic and copies ran while one was open for 8% of the time, Pallas kernels for 5%

profile of v1, /device:TPU:0, one launch (start us, length us, event | category | flops | bytes accessed | tf_op | source)
XLA Modules:
  0.0 323.6 jit_solution(8615359352061213585)
XLA Ops:
  0.0 0.8 reshape.664
  0.8 0.8 broadcast_in_dim_reshape.2
  1.5 1.4 reduce_sum.67
  3.0 0.1 reduce.3
  3.1 1.2 dynamic-slice
  4.3 1.4 dynamic-update-slice
  5.7 9.5 %all-reduce.1 = s32[8]{0:T(128)S(1)} all-reduce(s32[8]{0:T(128)S(1)} %dynamic-update-slice), channel_id=1, replica_groups=mesh['wide'=8,'narrow'=4] {'wide'}, use_global_device_ids=true, to_apply=%add.1 | all-reduce | flops 8 | bytes 64
  15.2 11.1 %while.13 = (s32[]{:T(128)}, s32[]{:T(128)}, s32[]{:T(128)}, s32[8]{0:T(128)S(1)}, s32[]{:T(128)}) while((s32[]{:T(128)}, s32[]{:T(128)}, s32[]{:T(128)}, s32[8]{0:T(128)S(1)}, s32[]{:T(128)}) %tuple.41), condition=%wide.region_2.3_spmd, body=%wide.region_1.2_spmd.sunk | while | flops 5 | bytes 115 | solution.py:52
  15.2 0.7 dynamic_slice.8
  16.5 0.7 dynamic_slice.8
  17.9 0.7 dynamic_slice.8
  19.3 0.7 dynamic_slice.8
  20.7 0.7 dynamic_slice.8
  22.1 0.7 dynamic_slice.8
  23.5 0.7 dynamic_slice.8
  24.9 0.7 dynamic_slice.8
  26.3 0.2 convert_reduce_fusion.2
  26.5 0.1 select_reduce_fusion
  26.6 0.7 convert_element_type.122
  27.3 3.3 %all-to-all-start = ((bf16[8,1,4]{2,1,0:T(2,128)(2,1)}), bf16[8,1,4]{2,1,0:T(2,128)(2,1)S(1)}, u32[]{:S(2)}, u32[]{:S(2)}) async-start(bf16[8,1,4]{2,1,0:T(2,128)(2,1)} %convert_element_type.122), calls=%async_computation | async-start | bytes 8192 | tf_op jit(solution)/shard_map/all_to_all | solution.py:317
  30.6 15.6 %shard_map.109 = bf16[16,32,1024]{2,1,0:T(8,128)(2,1)} custom-call(bf16[16,32,768]{2,1,0:T(8,128)(2,1)} %px_ref.1, bf16[768,1024]{1,0:T(8,128)(2,1)} %patch_ref.3, bf16[256,1024]{1,0:T(8,128)(2,1)} %pos_ref.3, f32[1,1024]{1,0:T(1,128)} %bitcast.41, bf16[1024,3072]{1,0:T(8,128)(2,1)} %qkv_ref.3, bf16[1024,1024]{1,0:T(8,128)(2,1)} %out_ref.3), custom_call_target="tpu_custom_call" | custom-call | flops 8000000000 | bytes 14000000 | tf_op jit(solution)/shard_map/pallas_call | solution.py:133
  46.2 0.9 fusion.39
  47.1 1.3 collective-permute-start.1
  48.4 3.0 collective-permute-start
  51.5 0.8 collective-permute-done
  52.3 1.1 pad_maximum_fusion.5
  53.5 1.3 collective-permute-start.3
  54.8 4.5 %collective-permute-start.2 = (bf16[18,1,1024]{2,1,0:T(2,128)(2,1)S(1)}, bf16[18,1,1024]{2,1,0:T(2,128)(2,1)S(1)}, u32[]{:S(2)}, u32[]{:S(2)}) collective-permute-start(bf16[18,1,1024]{2,1,0:T(2,128)(2,1)S(1)} %get-tuple-element.99), channel_id=1, source_target_pairs={{0,1},{1,2},{2,3},{4,5},{5,6},{6,7},{8,9},{9,10},{10,11},{12,13},{... | collective-permute-start | bytes 110600 | tf_op jit(solution)/shard_map/ppermute | solution.py:33
  59.5 0.2 collective-permute-done.3
  59.7 1.6 collective-permute-done.2
  61.3 2.0 pad_maximum_fusion
  63.3 0.1 slice.77
  63.6 0.2 pad_maximum_fusion.1
  63.8 0.5 slice.78
  64.2 0.2 broadcast_select_fusion.1
  64.5 0.7 convert_reduce_fusion
  65.2 0.3 reshape.629
  65.5 4.2 %fusion.2 = bf16[1536,1024]{1,0:T(8,128)(2,1)} fusion(bf16[612,1024]{1,0:T(8,128)(2,1)S(1)} %reshape.629, s32[1536]{0:T(1024)S(1)} %reshape.639), kind=kOutput, calls=%fused_computation.7 | convolution fusion | flops 1927698432 | bytes 4405248 | tf_op jit(solution)/shard_map/dot_general | solution.py:79
  69.8 7.6 %all-to-all-start.2 = ((bf16[32,48,1024]{2,1,0:T(8,128)(2,1)}), bf16[32,48,1024]{2,1,0:T(8,128)(2,1)}, u32[]{:S(2)}, u32[]{:S(2)}) async-start(bf16[32,48,1024]{2,1,0:T(8,128)(2,1)} %bitcast.32), calls=%async_computation.2 | async-start | bytes 6291456 | tf_op jit(solution)/shard_map/all_to_all | solution.py:328
  77.4 0.1 fusion.22
  77.5 10.9 %gather_fusion = bf16[32,256,768]{2,1,0:T(8,128)(2,1)} fusion(bf16[32,256,768]{2,1,0:T(8,128)(2,1)} %bitcast.31, s32[1024]{0:T(1024)S(1)} %pad_clamp_fusion.1), kind=kCustom, calls=%fused_computation | custom fusion | bytes 25165952 | tf_op jit(solution)/shard_map/gather | solution.py:316
  88.5 26.8 %all-to-all-done.2.rim_ref = bf16[32,48,1024]{2,1,0:T(8,128)(2,1)} async-done(((bf16[32,48,1024]{2,1,0:T(8,128)(2,1)}), bf16[32,48,1024]{2,1,0:T(8,128)(2,1)}, u32[]{:S(2)}, u32[]{:S(2)}) %all-to-all-start.2) | async-done | bytes 3145760 | tf_op jit(solution)/shard_map/all_to_all | solution.py:328
  115.3 5.5 %all-to-all-start.1 = ((bf16[32,256,768]{2,1,0:T(8,128)(2,1)}), bf16[32,256,768]{2,1,0:T(8,128)(2,1)}, u32[]{:S(2)}, u32[]{:S(2)}) async-start(bf16[32,256,768]{2,1,0:T(8,128)(2,1)} %gather_fusion), calls=%async_computation.1 | async-start | bytes 25165824 | tf_op jit(solution)/shard_map/all_to_all | solution.py:316
  121.0 0.2 mul.169
  121.2 0.1 copy.45
  121.5 0.1 fusion.23
  121.6 0.7 pad_maximum_fusion.6.lift_ref
  122.5 0.1 reduce.6
  122.7 0.7 select_reduce_fusion.1.where_ref
  123.5 0.5 fusion.4
  124.1 0.1 rsqrt.12
  124.2 0.7 reduce-precision_convert_fusion.1
  124.9 0.8 fusion.5
  125.8 0.4 reshape.634
  126.1 0.4 fusion.37
  126.5 133.3 %all-to-all-done.1.px_ref = bf16[32,256,768]{2,1,0:T(8,128)(2,1)} async-done(((bf16[32,256,768]{2,1,0:T(8,128)(2,1)}), bf16[32,256,768]{2,1,0:T(8,128)(2,1)}, u32[]{:S(2)}, u32[]{:S(2)}) %all-to-all-start.1) | async-done | bytes 12582944 | tf_op jit(solution)/shard_map/all_to_all | solution.py:316
  259.9 50.1 %shard_map.110 = bf16[7,16,256]{2,1,0:T(8,128)(2,1)} custom-call(s32[7]{0:T(128)} %select_reduce_fusion.1.where_ref, bf16[32,256,768]{2,1,0:T(8,128)(2,1)} %all-to-all-done.1.px_ref, bf16[32,48,1024]{2,1,0:T(8,128)(2,1)} %all-to-all-done.2.rim_ref, bf16[256,96]{1,0:T(8,128)(2,1)} %pad_maximum_fusion.6.lift_ref, bf16[768,1024]{1,0:T(8,128)(2,1)} %patch_ref.3, ...), custom_call_target="tpu_custom_call" | custom-call | flops 31499999232 | bytes 20000000 | tf_op jit(solution)/shard_map/pallas_call | solution.py:184
  310.0 0.8 copy.49
  310.8 0.3 convolution_convert_fusion
  311.1 0.8 copy.50
  311.9 3.4 %all-to-all-start.3 = ((bf16[32,16,256]{2,1,0:T(8,128)(2,1)}), bf16[32,16,256]{2,1,0:T(8,128)(2,1)S(1)}, u32[]{:S(2)}, u32[]{:S(2)}) async-start(bf16[32,16,256]{2,1,0:T(8,128)(2,1)} %bitcast.20), calls=%async_computation.3 | async-start | bytes 524288 | tf_op jit(solution)/shard_map/all_to_all | solution.py:350
  315.4 6.8 %all-to-all-done.3 = bf16[32,16,256]{2,1,0:T(8,128)(2,1)S(1)} async-done(((bf16[32,16,256]{2,1,0:T(8,128)(2,1)}), bf16[32,16,256]{2,1,0:T(8,128)(2,1)S(1)}, u32[]{:S(2)}, u32[]{:S(2)}) %all-to-all-start.3) | async-done | bytes 262176 | tf_op jit(solution)/shard_map/all_to_all | solution.py:350
  322.2 0.6 gather_fusion.1
  322.8 0.9 bitcast_select_fusion
  (43 shorter events, 1.2 us)
Async XLA Ops:
  27.3 42.5 %all-to-all-start = ((bf16[8,1,4]{2,1,0:T(2,128)(2,1)}), bf16[8,1,4]{2,1,0:T(2,128)(2,1)S(1)}, u32[]{:S(2)}, u32[]{:S(2)}) async-start(bf16[8,1,4]{2,1,0:T(2,128)(2,1)} %convert_element_type.122), calls=%async_computation | async-start | bytes 8192 | tf_op jit(solution)/shard_map/all_to_all | solution.py:317
  47.1 4.4 %collective-permute-start.1 = (bf16[1,32,1024]{2,1,0:T(8,128)(2,1)S(1)}, bf16[1,32,1024]{2,1,0:T(8,128)(2,1)S(1)}, u32[]{:S(2)}, u32[]{:S(2)}) collective-permute-start(bf16[1,32,1024]{2,1,0:T(8,128)(2,1)S(1)} %get-tuple-element.102), channel_id=1, source_target_pairs={{4,0},{8,4},{12,8},{16,12},{20,16},{24,20},{28,24},{5,1},{9,5},{13... | collective-permute-start | bytes 196616 | tf_op jit(solution)/shard_map/ppermute | solution.py:35
  48.4 3.9 %collective-permute-start = (bf16[1,32,1024]{2,1,0:T(8,128)(2,1)S(1)}, bf16[1,32,1024]{2,1,0:T(8,128)(2,1)S(1)}, u32[]{:S(2)}, u32[]{:S(2)}) collective-permute-start(bf16[1,32,1024]{2,1,0:T(8,128)(2,1)S(1)} %get-tuple-element.101), channel_id=1, source_target_pairs={{0,4},{4,8},{8,12},{12,16},{16,20},{20,24},{24,28},{1,5},{5,9},{9,... | collective-permute-start | bytes 196616 | tf_op jit(solution)/shard_map/ppermute | solution.py:33
  53.5 6.2 %collective-permute-start.3 = (bf16[18,1,1024]{2,1,0:T(2,128)(2,1)S(1)}, bf16[18,1,1024]{2,1,0:T(2,128)(2,1)S(1)}, u32[]{:S(2)}, u32[]{:S(2)}) collective-permute-start(bf16[18,1,1024]{2,1,0:T(2,128)(2,1)S(1)} %get-tuple-element.100), channel_id=1, source_target_pairs={{1,0},{2,1},{3,2},{5,4},{6,5},{7,6},{9,8},{10,9},{11,10},{13,12},{... | collective-permute-start | bytes 110600 | tf_op jit(solution)/shard_map/ppermute | solution.py:35
  54.8 6.5 %collective-permute-start.2 = (bf16[18,1,1024]{2,1,0:T(2,128)(2,1)S(1)}, bf16[18,1,1024]{2,1,0:T(2,128)(2,1)S(1)}, u32[]{:S(2)}, u32[]{:S(2)}) collective-permute-start(bf16[18,1,1024]{2,1,0:T(2,128)(2,1)S(1)} %get-tuple-element.99), channel_id=1, source_target_pairs={{0,1},{1,2},{2,3},{4,5},{5,6},{6,7},{8,9},{9,10},{10,11},{12,13},{... | collective-permute-start | bytes 110600 | tf_op jit(solution)/shard_map/ppermute | solution.py:33
  59.5 3.9 %copy-start = (bf16[16,32,1024]{2,1,0:T(8,128)(2,1)S(1)}, bf16[16,32,1024]{2,1,0:T(8,128)(2,1)}, u32[]{:S(2)}) copy-start(bf16[16,32,1024]{2,1,0:T(8,128)(2,1)} %shard_map.109) | copy-start | bytes 3145732
  69.8 45.6 %all-to-all-start.2 = ((bf16[32,48,1024]{2,1,0:T(8,128)(2,1)}), bf16[32,48,1024]{2,1,0:T(8,128)(2,1)}, u32[]{:S(2)}, u32[]{:S(2)}) async-start(bf16[32,48,1024]{2,1,0:T(8,128)(2,1)} %bitcast.32), calls=%async_computation.2 | async-start | bytes 6291456 | tf_op jit(solution)/shard_map/all_to_all | solution.py:328
  88.5 35.7 %copy-start.1 = (bf16[1024,16]{0,1:T(8,128)(2,1)S(1)}, bf16[1024,16]{0,1:T(8,128)(2,1)}, u32[]{:S(2)}) copy-start(bf16[1024,16]{0,1:T(8,128)(2,1)} %param.23) | copy-start | bytes 98308
  88.5 35.7 %copy-start.2 = (f32[1024]{0:T(1024)S(1)}, f32[1024]{0:T(1024)}, u32[]{:S(2)}) copy-start(f32[1024]{0:T(1024)} %param.22) | copy-start | bytes 12292
  115.3 144.5 %all-to-all-start.1 = ((bf16[32,256,768]{2,1,0:T(8,128)(2,1)}), bf16[32,256,768]{2,1,0:T(8,128)(2,1)}, u32[]{:S(2)}, u32[]{:S(2)}) async-start(bf16[32,256,768]{2,1,0:T(8,128)(2,1)} %gather_fusion), calls=%async_computation.1 | async-start | bytes 25165824 | tf_op jit(solution)/shard_map/all_to_all | solution.py:316
  311.9 10.3 %all-to-all-start.3 = ((bf16[32,16,256]{2,1,0:T(8,128)(2,1)}), bf16[32,16,256]{2,1,0:T(8,128)(2,1)S(1)}, u32[]{:S(2)}, u32[]{:S(2)}) async-start(bf16[32,16,256]{2,1,0:T(8,128)(2,1)} %bitcast.20), calls=%async_computation.3 | async-start | bytes 524288 | tf_op jit(solution)/shard_map/all_to_all | solution.py:350
